TPU v7x, 32 devices: a whole 2x2x4 slice. The times are simulated.
32 devices in a mesh: rep: 4 (over z), fsdp: 8 (over y, x, core).
Axes of the slice: x: 2, y: 2, z: 4, core: 2. Of those that a mesh axis runs over, the one named last changes fastest.
Arguments:
- layer_input: bfloat16 [16, 1024, 768], P('rep', 'fsdp'), may hold values from -40 to 40
- positions: int32 [16, 1024], P('rep', 'fsdp'), may hold values from 0 to 1023, as said below
- cotangent: bfloat16 [16, 1024, 768], P('rep', 'fsdp'), may hold values from -6 to 6
- w_qkv: bfloat16 [768, 2304], P('fsdp'), may hold values from -4 to 4
- w_out: bfloat16 [768, 768], P('fsdp'), may hold values from -1.75 to 1.75
- w_up: bfloat16 [768, 3072], P('fsdp'), may hold values from -0.21875 to 0.21875
- w_down: bfloat16 [768, 3072], P('fsdp'), may hold values from -0.109375 to 0.109375
- ln1_gain: bfloat16 [768], P('fsdp'), may hold values from 0.5 to 1.5
- ln1_bias: bfloat16 [768], P('fsdp'), may hold values from -1.5 to 1.5
- ln2_gain: bfloat16 [768], P('fsdp'), may hold values from 0.5 to 1.5
- ln2_bias: bfloat16 [768], P('fsdp'), may hold values from -1.5 to 1.5
- qkv_bias: bfloat16 [2304], P('fsdp'), may hold values from -2.5 to 2.5
- out_bias: bfloat16 [768], P('fsdp'), may hold values from -2.5 to 2.5
- up_bias: bfloat16 [3072], P('fsdp'), may hold values from -2.5 to 2.5
- down_bias: bfloat16 [768], P('fsdp'), may hold values from -2.5 to 2.5
Outputs:
- output: bfloat16 [16, 1024, 768], P('rep', 'fsdp')
- grad_input: bfloat16 [16, 1024, 768], P('rep', 'fsdp')
- grad_w_qkv: float32 [768, 2304], P('fsdp')
- grad_w_out: float32 [768, 768], P('fsdp')
- grad_w_up: float32 [768, 3072], P('fsdp')
- grad_w_down: float32 [768, 3072], P('fsdp')
- grad_ln1_gain: float32 [768], P('fsdp')
- grad_ln1_bias: float32 [768], P('fsdp')
- grad_ln2_gain: float32 [768], P('fsdp')
- grad_ln2_bias: float32 [768], P('fsdp')
- grad_qkv_bias: float32 [2304], P('fsdp')
- grad_out_bias: float32 [768], P('fsdp')
- grad_up_bias: float32 [3072], P('fsdp')
- grad_down_bias: float32 [768], P('fsdp')
Inputs may be any that keep to these rules, and one draw needn't show every extreme that they name: positions[s, 0] is 0, and each later positions[s, t] is either 0 or positions[s, t - 1] + 1; sequence 0 is one document of 1024 tokens.
All inputs are finite; a program needn't handle non-finite values.
Results may differ from a plain program's by a relative error of at most 0.0093.
Values may be sent and summed in bfloat16 or wider, within the bound.
No kernel may reach another device: no remote copies, remote signals or barrier semaphores. Data moves between devices by JAX's collectives and lax.ppermute only.
A program may use at most 320 MiB of HBM per device.

v0:
```python
import jax
import jax.numpy as jnp
from jax import lax
from jax.sharding import PartitionSpec as P

H = 12
HD = 64
ROT = 16
EPS = 1e-05
NEG = -1e30


def norm_rows(values, gain, shift):
    mean = jnp.mean(values, axis=-1, keepdims=True)
    centred = values - mean
    spread = jnp.mean(centred * centred, axis=-1, keepdims=True)
    return centred * lax.rsqrt(spread + EPS) * gain + shift


def rotate(values, cosine, sine):
    half = ROT // 2
    head = values[..., :ROT]
    turned = jnp.concatenate([-head[..., half:], head[..., :half]], axis=-1)
    return jnp.concatenate([head * cosine + turned * sine, values[..., ROT:]], axis=-1)


def angles(positions):
    inverse = 10000.0 ** (-jnp.arange(0, ROT, 2, dtype=jnp.float32) / ROT)
    phase = positions.astype(jnp.float32)[..., None] * inverse
    phase = jnp.concatenate([phase, phase], axis=-1)[..., None, :]
    return (jnp.cos(phase), jnp.sin(phase))


def on_device(
    layer_input,
    positions,
    cotangent,
    w_qkv,
    w_out,
    w_up,
    w_down,
    ln1_gain,
    ln1_bias,
    ln2_gain,
    ln2_bias,
    qkv_bias,
    out_bias,
    up_bias,
    down_bias,
):
    seq_count, span_len, width = layer_input.shape
    shard_count = lax.axis_size("fsdp")
    shard_index = lax.axis_index("fsdp")
    row_count = seq_count * span_len
    qkv_cols = w_qkv.shape[1]
    hidden_cols = w_up.shape[1]
    vectors = (
        lax.all_gather(ln1_gain, "fsdp", axis=0, tiled=True),
        lax.all_gather(ln1_bias, "fsdp", axis=0, tiled=True),
        lax.all_gather(ln2_gain, "fsdp", axis=0, tiled=True),
        lax.all_gather(ln2_bias, "fsdp", axis=0, tiled=True),
        lax.all_gather(qkv_bias, "fsdp", axis=0, tiled=True),
        lax.all_gather(out_bias, "fsdp", axis=0, tiled=True),
        lax.all_gather(up_bias, "fsdp", axis=0, tiled=True),
        lax.all_gather(down_bias, "fsdp", axis=0, tiled=True),
    )
    gain_one, shift_one, gain_two, shift_two, bias_qkv, bias_out, bias_up, bias_down = [
        v.astype(jnp.float32) for v in vectors
    ]
    source = layer_input.reshape(row_count, width).astype(jnp.float32)
    normed_one, pull_one = jax.vjp(norm_rows, source, gain_one, shift_one)
    normed_two, pull_two = jax.vjp(norm_rows, source, gain_two, shift_two)
    input_one = normed_one.astype(jnp.bfloat16)
    input_two = normed_two.astype(jnp.bfloat16)
    pieces = (
        lax.all_gather(w_qkv, "fsdp", axis=0, tiled=True),
        lax.all_gather(w_up, "fsdp", axis=0, tiled=True),
    )
    count = pieces[0].shape[0]
    qkv_sum = jnp.dot(input_one, pieces[0], preferred_element_type=jnp.float32)
    up_sum = jnp.dot(input_two, pieces[1], preferred_element_type=jnp.float32)
    qkv_full = qkv_sum + bias_qkv
    up_full = up_sum + bias_up
    cosine, sine = angles(positions)

    def turn_all(packed):
        shaped = packed.reshape(seq_count, span_len, 3, H, HD)
        return (
            rotate(shaped[:, :, 0], cosine, sine),
            rotate(shaped[:, :, 1], cosine, sine),
            shaped[:, :, 2],
        )

    turned, pull_turn = jax.vjp(turn_all, qkv_full)
    query_low = turned[0].astype(jnp.bfloat16)
    key_low = turned[1].astype(jnp.bfloat16)
    value_low = turned[2].astype(jnp.bfloat16)
    key_flat = key_low.reshape(seq_count, span_len, width)
    value_flat = value_low.reshape(seq_count, span_len, width)
    query_index = shard_index * span_len + jnp.arange(span_len, dtype=jnp.int32)
    first_seen = query_index[None, :] - positions

    def scores_with(key_piece):
        count = key_piece.shape[1]
        keys = key_piece.reshape(seq_count, count, H, HD)
        raw = (
            jnp.einsum("sqhd,skhd->shqk", query_low, keys, preferred_element_type=jnp.float32)
            * 0.125
        )
        key_index = jnp.arange(count, dtype=jnp.int32)
        seen = (key_index[None, None, :] <= query_index[None, :, None]) & (
            key_index[None, None, :] >= first_seen[:, :, None]
        )
        return (raw, seen[:, None])

    start_top = jnp.full((seq_count, H, span_len), NEG, jnp.float32)
    raw, seen = scores_with(lax.all_gather(key_flat, "fsdp", axis=1, tiled=True))
    masked = jnp.where(seen, raw, NEG)
    new_top = jnp.maximum(start_top, jnp.max(masked, axis=-1))
    weights = jnp.where(seen, jnp.exp(masked - new_top[..., None]), 0.0)
    total = jnp.sum(weights, axis=-1)
    log_total = new_top + jnp.log(total)
    pieces = (
        lax.all_gather(key_flat, "fsdp", axis=1, tiled=True),
        lax.all_gather(value_flat, "fsdp", axis=1, tiled=True),
    )
    raw, seen = scores_with(pieces[0])
    count = pieces[1].shape[1]
    values = pieces[1].reshape(seq_count, count, H, HD)
    probs = jnp.where(seen, jnp.exp(raw - log_total[..., None]), 0.0)
    probs_low = probs.astype(jnp.bfloat16)
    residue = (probs - probs_low.astype(jnp.float32)).astype(jnp.bfloat16)
    mixed_sum = jnp.einsum("shqk,skhd->sqhd", probs_low, values, preferred_element_type=jnp.float32)
    residue_sum = jnp.einsum("shqk,skhd->sqhd", residue, values, preferred_element_type=jnp.float32)
    attended = mixed_sum.reshape(row_count, width).astype(jnp.bfloat16)
    hidden = jax.nn.gelu(up_full, approximate=False).astype(jnp.bfloat16)
    pieces = (
        lax.all_gather(w_out, "fsdp", axis=0, tiled=True),
        lax.all_gather(w_down, "fsdp", axis=0, tiled=True),
    )
    columns = jnp.einsum("rk,ck->rc", attended, pieces[0], preferred_element_type=jnp.float32)
    columns = columns + jnp.einsum(
        "rk,ck->rc", hidden, pieces[1], preferred_element_type=jnp.float32
    )
    output = (
        (source + columns + bias_out + bias_down).astype(jnp.bfloat16).reshape(layer_input.shape)
    )
    grad_out = cotangent.reshape(row_count, width)
    pieces = (
        lax.all_gather(w_out, "fsdp", axis=0, tiled=True),
        lax.all_gather(w_down, "fsdp", axis=0, tiled=True),
    )
    count = pieces[0].shape[0]
    grad_attended = jnp.dot(grad_out, pieces[0], preferred_element_type=jnp.float32)
    grad_hidden = jnp.dot(grad_out, pieces[1], preferred_element_type=jnp.float32)
    grad_mixed = grad_attended.astype(jnp.bfloat16)
    gelu_value, pull_gelu = jax.vjp(lambda v: jax.nn.gelu(v, approximate=False), up_full)
    grad_up = pull_gelu(grad_hidden)[0].astype(jnp.bfloat16)
    grad_heads = grad_mixed.reshape(seq_count, span_len, H, HD)
    carried = jnp.sum(grad_heads.astype(jnp.float32) * (mixed_sum + residue_sum), axis=-1)
    carried_rows = jnp.transpose(carried, (0, 2, 1))
    pieces = (
        lax.all_gather(key_flat, "fsdp", axis=1, tiled=True),
        lax.all_gather(value_flat, "fsdp", axis=1, tiled=True),
    )
    raw, seen = scores_with(pieces[0])
    count = pieces[0].shape[1]
    keys = pieces[0].reshape(seq_count, count, H, HD)
    values = pieces[1].reshape(seq_count, count, H, HD)
    probs = jnp.where(seen, jnp.exp(raw - log_total[..., None]), 0.0)
    probs_low = probs.astype(jnp.bfloat16)
    grad_probs = jnp.einsum(
        "sqhd,skhd->shqk", grad_heads, values, preferred_element_type=jnp.float32
    )
    grad_scores = (probs * (grad_probs - carried_rows[..., None])).astype(jnp.bfloat16)
    grad_query = jnp.einsum(
        "shqk,skhd->sqhd", grad_scores, keys, preferred_element_type=jnp.float32
    )
    key_part = jnp.einsum(
        "shqk,sqhd->skhd", grad_scores, query_low, preferred_element_type=jnp.float32
    )
    value_part = jnp.einsum(
        "shqk,sqhd->skhd", probs_low, grad_heads, preferred_element_type=jnp.float32
    )
    both = jnp.concatenate(
        [key_part.reshape(seq_count, count, width), value_part.reshape(seq_count, count, width)],
        axis=2,
    )
    key_terms = both
    grad_query, key_terms = (grad_query, key_terms)
    grad_query = grad_query * 0.125
    key_owned = lax.psum_scatter(key_terms, "fsdp", scatter_dimension=1, tiled=True)
    grad_key = key_owned[..., :width].reshape(seq_count, span_len, H, HD) * 0.125
    grad_value = key_owned[..., width:].reshape(seq_count, span_len, H, HD)
    grad_qkv = pull_turn((grad_query, grad_key, grad_value))[0].astype(jnp.bfloat16)
    pieces = (
        lax.all_gather(w_qkv, "fsdp", axis=0, tiled=True),
        lax.all_gather(w_up, "fsdp", axis=0, tiled=True),
    )
    columns_one = jnp.einsum("rk,ck->rc", grad_qkv, pieces[0], preferred_element_type=jnp.float32)
    columns_two = jnp.einsum("rk,ck->rc", grad_up, pieces[1], preferred_element_type=jnp.float32)
    grad_source_one, grad_gain_one, grad_shift_one = pull_one(columns_one)
    grad_source_two, grad_gain_two, grad_shift_two = pull_two(columns_two)
    grad_out_float = grad_out.astype(jnp.float32)
    grad_input = (
        (grad_out_float + grad_source_one + grad_source_two)
        .astype(jnp.bfloat16)
        .reshape(layer_input.shape)
    )
    grad_out_total = jnp.sum(grad_out_float, axis=0)
    local_vectors = (
        grad_gain_one,
        grad_shift_one,
        grad_gain_two,
        grad_shift_two,
        jnp.sum(grad_qkv.astype(jnp.float32), axis=0),
        grad_out_total,
        jnp.sum(grad_up.astype(jnp.float32), axis=0),
    )
    summed = lax.psum(
        (
            local_vectors[0],
            local_vectors[1],
            local_vectors[2],
            local_vectors[3],
            local_vectors[4],
            local_vectors[5],
            local_vectors[6],
        ),
        ("rep", "fsdp"),
    )
    owned_vectors = [
        lax.dynamic_slice_in_dim(
            v, shard_index * (v.shape[0] // shard_count), v.shape[0] // shard_count
        )
        for v in summed
    ]
    owned = lax.psum_scatter(
        jnp.concatenate(
            [
                jnp.einsum("rc,rk->ck", input_one, grad_qkv, preferred_element_type=jnp.float32),
                jnp.einsum("rc,rk->ck", grad_out, attended, preferred_element_type=jnp.float32),
                jnp.einsum("rc,rk->ck", input_two, grad_up, preferred_element_type=jnp.float32),
                jnp.einsum("rc,rk->ck", grad_out, hidden, preferred_element_type=jnp.float32),
            ],
            axis=1,
        ),
        "fsdp",
        scatter_dimension=0,
        tiled=True,
    )
    owned = lax.psum(owned, "rep")
    edge_two = qkv_cols + width
    edge_three = edge_two + hidden_cols
    grad_w_qkv = owned[:, :qkv_cols]
    grad_w_out = owned[:, qkv_cols:edge_two]
    grad_w_up = owned[:, edge_two:edge_three]
    grad_w_down = owned[:, edge_three:]
    return (
        output,
        grad_input,
        grad_w_qkv,
        grad_w_out,
        grad_w_up,
        grad_w_down,
        owned_vectors[0],
        owned_vectors[1],
        owned_vectors[2],
        owned_vectors[3],
        owned_vectors[4],
        owned_vectors[5],
        owned_vectors[6],
        owned_vectors[5],
    )


def solution(mesh):
    return jax.shard_map(
        on_device,
        mesh=mesh,
        in_specs=(
            P("rep", "fsdp", None),
            P("rep", "fsdp"),
            P("rep", "fsdp", None),
            P("fsdp", None),
            P("fsdp", None),
            P("fsdp", None),
            P("fsdp", None),
            P("fsdp"),
            P("fsdp"),
            P("fsdp"),
            P("fsdp"),
            P("fsdp"),
            P("fsdp"),
            P("fsdp"),
            P("fsdp"),
        ),
        out_specs=(
            P("rep", "fsdp", None),
            P("rep", "fsdp", None),
            P("fsdp", None),
            P("fsdp", None),
            P("fsdp", None),
            P("fsdp", None),
            P("fsdp"),
            P("fsdp"),
            P("fsdp"),
            P("fsdp"),
            P("fsdp"),
            P("fsdp"),
            P("fsdp"),
            P("fsdp"),
        ),
        check_vma=False,
    )
```

profile of v0, /device:TPU:0, one launch (start us, length us, event | category | flops | bytes accessed | tf_op | source)
XLA Modules:
  0.0 780.7 jit_solution(14124956346842506521)
XLA Ops:
  8.7 1.3 convert_reduce_fusion.2
  10.1 1.5 fusion.28
  12.5 1.2 dynamic-slice
  15.1 0.8 dynamic-update-slice
  15.9 0.8 dynamic-update-slice.1
  16.8 0.8 dynamic-update-slice.3
  18.4 0.8 dynamic-update-slice.5
  19.3 0.8 dynamic-update-slice.6
  20.1 0.9 dynamic-update-slice.2
  21.0 26.5 %all-reduce.19 = (bf16[768]{0:T(1024)(128)(2,1)S(1)}, bf16[768]{0:T(1024)(128)(2,1)S(1)}, bf16[768]{0:T(1024)(128)(2,1)}, bf16[768]{0:T(1024)(128)(2,1)}, bf16[7...) all-reduce(bf16[768]{0:T(1024)(128)(2,1)S(1)} %dynamic-update-slice, ...), channel_id=1, replica_groups=mesh['rep'=4,'fsdp'=8] {'fsdp'}, use_global_device_ids=true, to_apply=%add.15 | all-reduce | flops 6912 | bytes 27648
  47.6 1.6 fusion.33
  49.2 6.1 convolution_add_fusion
  55.4 6.2 copy.46
  61.5 6.3 reshape.249
  67.9 2.2 fusion.78
  70.7 1.0 copy-done.7
  71.8 1.0 pad_maximum_fusion.3
  72.9 1.7 slice.108
  74.6 1.1 copy.47
  77.7 2.9 convolution_convert_fusion
  80.6 1.5 copy.51
  82.1 1.1 reshape.254
  83.2 1.4 slice.110
  84.6 37.4 %all-gather.12.cloned.1.call-done = bf16[4,1024,768]{1,2,0:T(8,128)(2,1)} async-done(((bf16[4,128,768]{1,2,0:T(8,128)(2,1)}), bf16[4,1024,768]{1,2,0:T(8,128)(2,1)}) %all-gather.12.cloned.1.call-update) | async-done | bytes 6291472 | tf_op jit(solution)/shard_map/all_gather | solution.py:124
  121.9 12.9 %select_reduce_fusion.1 = (f32[4,12,128]{2,1,0:T(8,128)S(1)}, f32[4,12,128,1024]{3,2,1,0:T(8,128)}) fusion(pred[4,128,1024]{2,1,0:T(8,128)(4,1)S(1)} %fusion.13, bf16[4,1024,12,64]{1,3,2,0:T(8,128)(2,1)} %bitcast.164, bf16[4,128,12,48]{1,3,2,0:T(8,128)(2,1)S(1)} %slice.110, bf16[4,128,12,16]{1,3,2,0:T(8,128)(2,1)S(1)} %get-tuple-element.61), kind=kOutput, calls=%fused_computation.6 | convolution fusion | flops 825747456 | bytes 32792576 | tf_op jit(solution)/shard_map/sqhd,skhd->shqk/dot_general | solution.py:107
  134.9 12.2 %select_reduce_fusion = f32[4,12,128]{2,1,0:T(8,128)S(1)} fusion(f32[4,12,128,1024]{3,2,1,0:T(8,128)} %get-tuple-element.76, f32[4,12,128]{2,1,0:T(8,128)S(1)} %broadcast_maximum_fusion, pred[4,128,1024]{2,1,0:T(8,128)(4,1)S(1)} %fusion.13), kind=kLoop, calls=%fused_computation.5 | loop fusion | flops 31451136 | bytes 25739264 | tf_op jit(solution)/shard_map/reduce_sum | solution.py:121
  147.1 23.9 %all-gather.10.cloned.1.call-done = bf16[4,1024,768]{1,2,0:T(8,128)(2,1)} async-done(((bf16[4,128,768]{1,2,0:T(8,128)(2,1)}), bf16[4,1024,768]{1,2,0:T(8,128)(2,1)}) %all-gather.10.cloned.1.call-update) | async-done | bytes 6291472 | tf_op jit(solution)/shard_map/all_gather | solution.py:125
  170.9 14.2 %fusion.58 = f32[4,12,64,128]{3,2,1,0:T(8,128)} fusion(bf16[4,1024,12,64]{1,3,2,0:T(8,128)(2,1)} %bitcast.190, f32[4,12,128,1024]{3,2,1,0:T(8,128)} %get-tuple-element.76, f32[4,12,128]{2,1,0:T(8,128)S(1)} %log_add_fusion, pred[4,128,1024]{2,1,0:T(8,128)(4,1)S(1)} %fusion.13), kind=kOutput, calls=%fused_computation.110 | convolution fusion | flops 830472192 | bytes 33579008 | tf_op jit(solution)/shard_map/shqk,skhd->sqhd/dot_general | solution.py:133
  185.2 15.0 %fusion.16 = f32[4,128,12]{1,2,0:T(8,128)S(1)} fusion(f32[4,12,64,128]{3,2,1,0:T(8,128)} %fusion.58, bf16[4,1024,12,64]{1,3,2,0:T(8,128)(2,1)} %bitcast.191, f32[4,12,128,1024]{3,2,1,0:T(8,128)} %get-tuple-element.76, f32[4,12,128]{2,1,0:T(8,128)S(1)} %log_add_fusion, pred[4,128,1024]{2,1,0:T(8,128)(4,1)S(1)} %fusion.13, bf16[4,128,12,64]{1,0,3,2:T(4,128)(2,1)} %reshape.254), kind=kOutput, calls=%fused_computation.48 | convolution fusion | flops 850913280 | bytes 34390016 | tf_op jit(solution)/shard_map/shqk,skhd->sqhd/dot_general | solution.py:134
  200.2 20.5 %multiply_convert_fusion = bf16[4,12,128,1024]{3,2,1,0:T(8,128)(2,1)} fusion(f32[4,12,128,1024]{3,2,1,0:T(8,128)} %get-tuple-element.76, f32[4,12,128]{2,1,0:T(8,128)S(1)} %bitcast.194, f32[4,12,128]{2,1,0:T(8,128)S(1)} %log_add_fusion, pred[4,128,1024]{2,1,0:T(8,128)(4,1)S(1)} %fusion.13, bf16[4,1024,12,64]{1,3,2,0:T(8,128)(2,1)} %bitcast.192, ...), kind=kOutput, calls=%fused_computation.2 | convolution fusion | flops 843055104 | bytes 45400064 | tf_op jit(solution)/shard_map/sqhd,skhd->shqk/dot_general | solution.py:172
  220.6 11.1 %fusion.50 = f32[4,12,64,1024]{3,2,1,0:T(8,128)} fusion(bf16[4,12,128,1024]{3,2,1,0:T(8,128)(2,1)} %multiply_convert_fusion, bf16[4,128,12,48]{1,3,2,0:T(8,128)(2,1)S(1)} %slice.110, bf16[4,128,12,16]{1,3,2,0:T(8,128)(2,1)S(1)} %get-tuple-element.61), kind=kOutput, calls=%fused_computation.98 | convolution fusion | flops 806879232 | bytes 25952256 | tf_op jit(solution)/shard_map/shqk,sqhd->skhd/dot_general | solution.py:179
  231.8 14.8 %fusion.47 = f32[4,12,64,1024]{3,2,1,0:T(8,128)} fusion(bf16[4,128,12,64]{1,0,3,2:T(4,128)(2,1)S(1)} %copy-done.12, f32[4,12,128,1024]{3,2,1,0:T(8,128)} %get-tuple-element.76, f32[4,12,128]{2,1,0:T(8,128)S(1)} %log_add_fusion, pred[4,128,1024]{2,1,0:T(8,128)(4,1)S(1)} %fusion.13), kind=kOutput, calls=%fused_computation.94 | convolution fusion | flops 830472192 | bytes 39084032 | tf_op jit(solution)/shard_map/shqk,sqhd->skhd/dot_general | solution.py:182
  246.5 18.8 %pad_maximum_fusion.1 = f32[4,1024,1536]{1,2,0:T(8,128)} fusion(f32[4,1024,768]{1,2,0:T(8,128)} %bitcast.163, f32[4,1024,768]{1,2,0:T(8,128)} %bitcast.162), kind=kLoop, calls=%fused_computation.1 | loop fusion | flops 6291456 | bytes 50331648 | tf_op jit(solution)/shard_map/concatenate | solution.py:185
  266.0 9.4 %all-gather = bf16[8,1,384]{2,1,0:T(2,128)(2,1)S(1)} all-gather(bf16[1,1,384]{2,1,0:T(2,128)(2,1)S(1)} %reshape.280), channel_id=1, replica_groups=mesh['rep'=4,'fsdp'=8] {'fsdp'}, dimensions={0}, use_global_device_ids=true | all-gather | bytes 6912 | tf_op jit(solution)/shard_map/all_gather | solution.py:64
  275.5 1.2 fusion.31
  276.7 8.9 %fusion.83 = f32[512,3072]{1,0:T(8,128)} fusion(bf16[512,768]{1,0:T(8,128)(2,1)S(1)} %get-tuple-element.54, bf16[768,3072]{1,0:T(8,128)(2,1)} %all-gather.16.cloned.1.call-done), kind=kOutput, calls=%fused_computation.154 | convolution fusion | flops 2415919104 | bytes 11796480 | tf_op jit(solution)/shard_map/dot_general | solution.py:81
  285.6 19.4 %convert_reduce_fusion = (f32[3072]{0:T(1024)S(1)}, bf16[512,3072]{1,0:T(8,128)(2,1)S(1)}, f32[512,3072]{1,0:T(8,128)S(1)}) fusion(f32[512,3072]{1,0:T(8,128)} %fusion.83, f32[3072]{0:T(1024)S(1)} %bitcast.188, bf16[512,768]{1,0:T(8,128)(2,1)S(1)} %bitcast.170, bf16[768,3072]{1,0:T(8,128)(2,1)} %all-gather.18.cloned.1.call-done), kind=kOutput, calls=%fused_computation.12 | convolution fusion | flops 2533880832 | bytes 21258240 | tf_op jit(solution)/shard_map/dot_general | solution.py:155
  305.0 3.2 multiply_convert_fusion.1
  308.2 7.8 convolution_bitcast_fusion
  316.0 5.2 fusion.86
  321.2 11.3 %multiply_bitcast_fusion = f32[4,128,12,64]{1,3,2,0:T(8,128)S(1)} fusion(bf16[4,1024,12,64]{1,3,2,0:T(8,128)(2,1)} %bitcast.165, bf16[4,12,128,1024]{3,2,1,0:T(8,128)(2,1)} %multiply_convert_fusion), kind=kOutput, calls=%fused_computation.82 | convolution fusion | flops 805699584 | bytes 20447232 | tf_op jit(solution)/shard_map/shqk,skhd->sqhd/dot_general | solution.py:176
  332.5 2.3 convert_bitcast_fusion
  335.5 0.9 copy-done.9
  336.3 2.2 convolution_bitcast_fusion.1
  338.5 2.0 copy.57
  340.6 82.4 %reduce-scatter.3.cloned.1.call-done = f32[4,128,1536]{1,2,0:T(8,128)} async-done(((f32[4,1024,1536]{1,2,0:T(8,128)}), f32[4,128,1536]{1,2,0:T(8,128)}) %reduce-scatter.3.cloned.1.call-update) | async-done | bytes 3145744 | tf_op jit(solution)/shard_map/reduce_scatter | solution.py:192
  423.0 2.2 fusion.80
  427.4 2.2 copy.55
  429.7 1.5 copy-done.13
  431.2 4.9 fusion.9
  436.1 19.4 %pad_maximum_fusion = f32[768,9216]{1,0:T(8,128)} fusion(f32[768,3072]{1,0:T(8,128)} %convolution_bitcast_fusion, f32[768,3072]{1,0:T(8,128)} %fusion.86, f32[768,768]{1,0:T(8,128)S(1)} %copy.57, f32[768,2304]{1,0:T(8,128)} %fusion.9), kind=kLoop, calls=%fused_computation | loop fusion | flops 21233664 | bytes 56623104 | tf_op jit(solution)/shard_map/concatenate | solution.py:239
  456.4 172.6 %reduce-scatter.5.cloned.1.call-done = f32[96,9216]{1,0:T(8,128)} async-done(((f32[768,9216]{1,0:T(8,128)}), f32[96,9216]{1,0:T(8,128)}) %reduce-scatter.5.cloned.1.call-update) | async-done | bytes 3538960 | tf_op jit(solution)/shard_map/reduce_scatter | solution.py:238
  629.0 6.1 fusion.85
  635.1 5.8 fusion.84
  641.0 1.8 fusion.42
  642.9 5.4 fusion.76
  648.3 1.1 copy-done.6
  649.4 1.4 fusion.37
  650.8 44.4 %all-reduce.18 = (f32[768]{0:T(1024)S(1)}, f32[768]{0:T(1024)S(1)}, f32[768]{0:T(1024)S(1)}, f32[768]{0:T(1024)S(1)}, f32[2304]{0:T(1024)S(1)}, /*index=5*/f32[768]{0:T(1024)S(1)}, f32[3072]{0:T(1024)S(1)}) all-reduce(f32[768]{0:T(1024)S(1)} %get-tuple-element.23, ...), channel_id=1, replica_groups=mesh['rep'=4,'fsdp'=8] {'rep','fsdp'}, use_global_device_ids=true, to_apply=%region_13.14 | all-reduce | flops 9216 | bytes 73728 | tf_op jit(solution)/shard_map/psum | solution.py:220
  698.9 3.0 add_convert_fusion.2
  701.9 64.2 %all-reduce.22.cloned.1.call-done = f32[96,9216]{1,0:T(8,128)} async-done(((f32[96,9216]{1,0:T(8,128)}), f32[96,9216]{1,0:T(8,128)}) %all-reduce.22.cloned.1.call-update) | async-done | bytes 3538960 | tf_op jit(solution)/shard_map/psum | solution.py:252
  766.1 3.3 fusion.79
  769.4 2.1 slice.88
  771.5 1.7 slice.89
  (144 shorter events, 14.8 us)
Async XLA Ops:
  7.2 42.0 %all-gather.8.cloned.1.call-start = ((), (), s32[]{:S(2)}) async-start(), calls=%async_computation.2 | async-start | bytes 3981312 | tf_op jit(solution)/shard_map/all_gather | solution.py:76
  7.9 69.8 %all-gather.14.cloned.1.call-start = ((), (), s32[]{:S(2)}) async-start(), calls=%async_computation.5 | async-start | bytes 1327104 | tf_op jit(solution)/shard_map/all_gather | solution.py:138
  8.7 113.3 %all-gather.12.cloned.1.call-start = ((), (), s32[]{:S(2)}) async-start(), calls=%async_computation.4 | async-start | bytes 7077888 | tf_op jit(solution)/shard_map/all_gather | solution.py:124
  10.0 45.3 %copy-start.23 = (f32[512]{0:T(512)}, f32[512]{0:T(512)S(1)}, u32[]{:S(2)}) copy-start(f32[512]{0:T(512)S(1)} %get-tuple-element.73) | copy-start | bytes 6148
  11.6 263.9 %copy-start.27 = (f32[4,128]{1,0:T(4,128)}, f32[4,128]{1,0:T(4,128)S(1)}, u32[]{:S(2)}) copy-start(f32[4,128]{1,0:T(4,128)S(1)} %fusion.28) | copy-start | bytes 6148
  12.5 58.2 %copy-start.15 = (f32[4,128,16]{1,2,0:T(8,128)}, f32[4,128,16]{1,2,0:T(8,128)S(1)}, u32[]{:S(2)}) copy-start(f32[4,128,16]{1,2,0:T(8,128)S(1)} %get-tuple-element.67) | copy-start | bytes 98308
  12.5 58.2 %copy-start.17 = (f32[4,128,16]{1,2,0:T(8,128)}, f32[4,128,16]{1,2,0:T(8,128)S(1)}, u32[]{:S(2)}) copy-start(f32[4,128,16]{1,2,0:T(8,128)S(1)} %get-tuple-element.68) | copy-start | bytes 98308
  47.5 228.0 %copy-start.19 = (f32[768]{0:T(1024)}, f32[768]{0:T(1024)S(1)}, u32[]{:S(2)}) copy-start(f32[768]{0:T(1024)S(1)} %convert_element_type.126) | copy-start | bytes 9220
  47.5 7.9 %copy-start.21 = (f32[768]{0:T(1024)}, f32[768]{0:T(1024)S(1)}, u32[]{:S(2)}) copy-start(f32[768]{0:T(1024)S(1)} %convert_element_type.137) | copy-start | bytes 9220
  47.6 7.8 copy-start.25
  70.5 1.2 copy-start.7
  71.7 6.0 copy-start.5
  72.8 98.1 %all-gather.10.cloned.1.call-start = ((), (), s32[]{:S(2)}) async-start(), calls=%async_computation.3 | async-start | bytes 7077888 | tf_op jit(solution)/shard_map/all_gather | solution.py:125
  75.6 201.1 %all-gather.16.cloned.1.call-start = ((), (), s32[]{:S(2)}) async-start(), calls=%async_computation.6 | async-start | bytes 5308416 | tf_op jit(solution)/shard_map/all_gather | solution.py:77
  76.2 209.3 %all-gather.18.cloned.1.call-start = ((), (), s32[]{:S(2)}) async-start(), calls=%async_computation.7 | async-start | bytes 5308416 | tf_op jit(solution)/shard_map/all_gather | solution.py:139
  76.8 346.2 %reduce-scatter.3.cloned.1.call-start = ((), (), s32[]{:S(2)}) async-start(), calls=%async_computation.8 | async-start | bytes 28311552 | tf_op jit(solution)/shard_map/reduce_scatter | solution.py:192
  220.6 11.1 %copy-start.12 = (bf16[4,128,12,64]{1,0,3,2:T(4,128)(2,1)S(1)}, bf16[4,128,12,64]{1,0,3,2:T(4,128)(2,1)}, u32[]{:S(2)}) copy-start(bf16[4,128,12,64]{1,0,3,2:T(4,128)(2,1)} %reshape.254) | copy-start | bytes 2359300
  265.3 0.7 copy-start.31
  265.3 10.1 %copy-start = (bf16[4,128,768]{2,1,0:T(8,128)(2,1)S(1)}, bf16[4,128,768]{2,1,0:T(8,128)(2,1)}, u32[]{:S(2)}) copy-start(bf16[4,128,768]{2,1,0:T(8,128)(2,1)} %param.15) | copy-start | bytes 2359300
  265.3 363.6 %reduce-scatter.5.cloned.1.call-start = ((), (), s32[]{:S(2)}) async-start(), calls=%async_computation.9 | async-start | bytes 31850496 | tf_op jit(solution)/shard_map/reduce_scatter | solution.py:238
  285.6 19.4 %copy-start.2 = (f32[512,3072]{1,0:T(8,128)S(1)}, f32[512,3072]{1,0:T(8,128)}, u32[]{:S(2)}) copy-start(f32[512,3072]{1,0:T(8,128)} %fusion.83) | copy-start | bytes 18874372
  305.0 11.0 %copy-start.8 = (bf16[512,3072]{1,0:T(8,128)(2,1)}, bf16[512,3072]{1,0:T(8,128)(2,1)S(1)}, u32[]{:S(2)}) copy-start(bf16[512,3072]{1,0:T(8,128)(2,1)S(1)} %get-tuple-element.39) | copy-start | bytes 9437188
  332.5 3.0 copy-start.3
  335.5 0.9 copy-start.9
  338.5 86.7 %copy-start.18 = (f32[4,128,16]{1,2,0:T(8,128)S(1)}, f32[4,128,16]{1,2,0:T(8,128)}, u32[]{:S(2)}) copy-start(f32[4,128,16]{1,2,0:T(8,128)} %copy-done.17) | copy-start | bytes 98308
  340.6 85.1 %copy-start.16 = (f32[4,128,16]{1,2,0:T(8,128)S(1)}, f32[4,128,16]{1,2,0:T(8,128)}, u32[]{:S(2)}) copy-start(f32[4,128,16]{1,2,0:T(8,128)} %copy-done.15) | copy-start | bytes 98308
  423.0 2.4 copy-start.4
  425.5 1.3 slice-start
  427.0 4.2 copy-start.14
  429.7 1.5 copy-start.13
  455.5 0.7 copy-start.30
  455.5 0.7 copy-start.29
  455.5 310.6 %all-reduce.22.cloned.1.call-start = ((), (), s32[]{:S(2)}) async-start(), calls=%async_computation.10 | async-start | bytes 7077888 | tf_op jit(solution)/shard_map/psum | solution.py:252
  629.0 6.1 copy-start.11
  635.1 5.9 copy-start.1
  635.1 5.9 copy-start.10
  635.1 5.9 copy-start.32
  641.0 1.9 copy-start.20
  641.0 1.9 copy-start.22
  641.0 1.9 copy-start.24
  642.9 5.4 copy-start.28
  642.9 6.5 copy-start.26
  648.2 1.2 copy-start.6
  695.3 78.0 %copy-start.33 = (f32[96]{0:T(128)}, f32[96]{0:T(128)S(1)}, u32[]{:S(2)}) copy-start(f32[96]{0:T(128)S(1)} %dynamic_slice.26) | copy-start | bytes 1156
Sparse Core Ops, SparseCore 0:
  9.9 36.8 all-gather.7
  48.7 24.0 all-gather.13
  75.2 46.6 all-gather.11
  124.2 46.6 all-gather.9
  172.7 38.9 all-gather.15
  213.4 38.8 all-gather.17
  265.5 157.4 reduce-scatter.2
  455.7 173.2 reduce-scatter.4
  631.3 134.7 all-reduce.21
where the time goes:
time: 787 us; the launch traced here: 781 us
  waiting for transfers between devices  383 us (49%)
  matrix products  176 us (22%)
  blocking collectives  80.3 us (10%)
  other arithmetic  72.3 us (9%)
  local copies, waits for them, and re-layouts  51.7 us (7%)
  between operations  16.3 us (2%)
    reduce_scatter x1, waiting for transfers between devices, on_device(): lax.psum_scatter(jnp.concatenate([jnp.einsum('rc,rk->ck', input_one, grad...  173 us
    reduce_scatter x1, waiting for transfers between devices, on_device(): lax.psum_scatter(key_terms, 'fsdp', scatter_dimension=1, tiled=True)  82.4 us
    psum x1, waiting for transfers between devices, on_device(): owned = lax.psum(owned, 'rep')  64.2 us
    psum x1, blocking collectives, on_device(): lax.psum((local_vectors[0], local_vectors[1], local_vectors[2], local_vec...  44.4 us
    all_gather x1, waiting for transfers between devices, on_device(): lax.all_gather(key_flat, 'fsdp', axis=1, tiled=True)  37.4 us
    unnamed x1, blocking collectives  26.5 us
    all_gather x1, waiting for transfers between devices, on_device(): lax.all_gather(value_flat, 'fsdp', axis=1, tiled=True)  23.9 us
    dot_general x1, matrix products, on_device(): jnp.einsum('sqhd,skhd->shqk', grad_heads, values, preferred_element_type=...  20.5 us
  transfers between devices with their start and end apart: 9, of which 5 were waited for; matrix products, arithmetic and copies ran while one was open for 33% of the time, Pallas kernels for 0%

commit v1 on v0

--- a/solution.py
+++ b/solution.py
@@ -1,3 +1,4 @@
+import functools
 import jax
 import jax.numpy as jnp
 from jax import lax
@@ -8,6 +9,24 @@
 ROT = 16
 EPS = 1e-05
 NEG = -1e30
+
+
+def end_slices_on(original, pos_dim):
+    n_all = jax.lax.axis_size("fsdp")
+    found = [original]
+    p = 1
+    while p < n_all:
+        found.append(
+            jax.lax.ppermute(
+                found[p - 1], "fsdp", [(idx, (idx - 1) % n_all) for idx in range(n_all)]
+            )
+        )
+        p += 1
+    s_next = jnp.concatenate(found, pos_dim)
+    return jnp.roll(s_next, jax.lax.axis_index("fsdp") * original.shape[pos_dim], pos_dim)
+
+
+change_patches_over_axis = functools.partial(end_slices_on, pos_dim=1)
 
 
 def norm_rows(values, gain, shift):
@@ -121,7 +140,7 @@
     total = jnp.sum(weights, axis=-1)
     log_total = new_top + jnp.log(total)
     pieces = (
-        lax.all_gather(key_flat, "fsdp", axis=1, tiled=True),
+        change_patches_over_axis(key_flat),
         lax.all_gather(value_flat, "fsdp", axis=1, tiled=True),
     )
     raw, seen = scores_with(pieces[0])

time: 787 us -> 877 us (1.11)
  local copies, waits for them, and re-layouts: 51.7 us -> 84.7 us
  waiting for transfers between devices: 383 us -> 411 us
  starting transfers between devices: 0.82 us -> 17.6 us
  matrix products: 176 us -> 185 us
    ppermute x0 -> x7, waiting for transfers between devices: none -> 88 us  [end_slices_on(): jax.lax.ppermute(found[p - 1], 'fsdp', [(idx, (idx - 1) % n_all) for idx...]
    all_gather x1, waiting for transfers between devices: 37.4 us -> 0.01 us  [on_device(): lax.all_gather(key_flat, 'fsdp', axis=1, tiled=True)]
    unnamed x87 -> x118, local copies, waits for them, and re-layouts: 13.7 us -> 39.8 us
    all_gather x1, waiting for transfers between devices: 23.9 us -> 0.02 us  [on_device(): lax.all_gather(value_flat, 'fsdp', axis=1, tiled=True)]
    ppermute x0 -> x7, starting transfers between devices: none -> 17 us  [end_slices_on(): jax.lax.ppermute(found[p - 1], 'fsdp', [(idx, (idx - 1) % n_all) for idx...]
    dot_general x1 -> x2, matrix products: 12.9 us -> 23.4 us  [scores_with(): jnp.einsum('sqhd,skhd->shqk', query_low, keys, preferred_element_type=jnp...]
  transfers between devices with their start and end apart: 9 -> 16, of which waited for: 5 -> 10; matrix products, arithmetic and copies ran while one was open for 33% -> 34% of each run, Pallas kernels for 0% -> 0%
where the time goes in v1:
time: 877 us; the launch traced here: 867 us
  waiting for transfers between devices  411 us (47%)
  matrix products  185 us (21%)
  local copies, waits for them, and re-layouts  84.7 us (10%)
  blocking collectives  79.8 us (9%)
  other arithmetic  72.7 us (8%)
  starting transfers between devices  17.6 us (2%)
  between operations  16.4 us (2%)
    reduce_scatter x1, waiting for transfers between devices, on_device(): lax.psum_scatter(jnp.concatenate([jnp.einsum('rc,rk->ck', input_one, grad...  173 us
    ppermute x7, waiting for transfers between devices, end_slices_on(): jax.lax.ppermute(found[p - 1], 'fsdp', [(idx, (idx - 1) % n_all) for idx...  88 us
    reduce_scatter x1, waiting for transfers between devices, on_device(): lax.psum_scatter(key_terms, 'fsdp', scatter_dimension=1, tiled=True)  84.1 us
    psum x1, waiting for transfers between devices, on_device(): owned = lax.psum(owned, 'rep')  64.2 us
    psum x1, blocking collectives, on_device(): lax.psum((local_vectors[0], local_vectors[1], local_vectors[2], local_vec...  44.4 us
    unnamed x118, local copies, waits for them, and re-layouts  39.8 us
    unnamed x1, blocking collectives  26.5 us
    dot_general x2, matrix products, scores_with(): jnp.einsum('sqhd,skhd->shqk', query_low, keys, preferred_element_type=jnp...  23.4 us
  transfers between devices with their start and end apart: 16, of which 10 were waited for; matrix products, arithmetic and copies ran while one was open for 34% of the time, Pallas kernels for 0%

profile of v1, /device:TPU:0, one launch (start us, length us, event | category | flops | bytes accessed | tf_op | source)
XLA Modules:
  0.0 867.5 jit_solution(344869509888427410)
XLA Ops:
  21.0 26.5 %all-reduce.19 = (bf16[768]{0:T(1024)(128)(2,1)S(1)}, bf16[768]{0:T(1024)(128)(2,1)S(1)}, bf16[768]{0:T(1024)(128)(2,1)}, bf16[768]{0:T(1024)(128)(2,1)}, bf16[7...) all-reduce(bf16[768]{0:T(1024)(128)(2,1)S(1)} %dynamic-update-slice, ...), channel_id=1, replica_groups=mesh['rep'=4,'fsdp'=8] {'fsdp'}, use_global_device_ids=true, to_apply=%add.15 | all-reduce | flops 6912 | bytes 27648
  49.2 6.1 convolution_add_fusion
  55.4 6.2 copy.46
  61.5 6.4 reshape.251
  67.9 2.2 fusion.88
  77.0 16.3 %collective-permute-done = bf16[4,128,768]{1,2,0:T(8,128)(2,1)S(1)} collective-permute-done((bf16[4,128,768]{1,2,0:T(8,128)(2,1)}, bf16[4,128,768]{1,2,0:T(8,128)(2,1)S(1)}, u32[]{:S(2)}, u32[]{:S(2)}) %collective-permute-start) | collective-permute-done | bytes 786464 | tf_op jit(solution)/shard_map/ppermute | solution.py:20
  93.3 2.7 collective-permute-start.1
  96.1 9.5 %collective-permute-done.1 = bf16[4,128,768]{1,2,0:T(8,128)(2,1)S(1)} collective-permute-done((bf16[4,128,768]{1,2,0:T(8,128)(2,1)S(1)}, bf16[4,128,768]{1,2,0:T(8,128)(2,1)S(1)}, u32[]{:S(2)}, u32[]{:S(2)}) %collective-permute-start.1) | collective-permute-done | bytes 786464 | tf_op jit(solution)/shard_map/ppermute | solution.py:20
  106.5 2.8 collective-permute-start.2
  109.3 26.1 %collective-permute-done.2 = bf16[4,128,768]{1,2,0:T(8,128)(2,1)S(1)} collective-permute-done((bf16[4,128,768]{1,2,0:T(8,128)(2,1)S(1)}, bf16[4,128,768]{1,2,0:T(8,128)(2,1)S(1)}, u32[]{:S(2)}, u32[]{:S(2)}) %collective-permute-start.2) | collective-permute-done | bytes 786464 | tf_op jit(solution)/shard_map/ppermute | solution.py:20
  136.3 2.8 collective-permute-start.3
  139.1 9.5 %collective-permute-done.3 = bf16[4,128,768]{1,2,0:T(8,128)(2,1)} collective-permute-done((bf16[4,128,768]{1,2,0:T(8,128)(2,1)S(1)}, bf16[4,128,768]{1,2,0:T(8,128)(2,1)}, u32[]{:S(2)}, u32[]{:S(2)}) %collective-permute-start.3) | collective-permute-done | bytes 786464 | tf_op jit(solution)/shard_map/ppermute | solution.py:20
  148.6 2.9 collective-permute-start.4
  151.6 16.9 %collective-permute-done.4 = bf16[4,128,768]{1,2,0:T(8,128)(2,1)} collective-permute-done((bf16[4,128,768]{1,2,0:T(8,128)(2,1)}, bf16[4,128,768]{1,2,0:T(8,128)(2,1)}, u32[]{:S(2)}, u32[]{:S(2)}) %collective-permute-start.4) | collective-permute-done | bytes 786464 | tf_op jit(solution)/shard_map/ppermute | solution.py:20
  168.5 2.9 collective-permute-start.5
  172.0 2.9 convolution_convert_fusion
  174.9 2.3 copy.51
  177.2 2.4 reshape.257
  182.1 4.7 collective-permute-done.5
  186.8 2.8 collective-permute-start.6
  189.7 2.2 constant_dynamic-update-slice_fusion.14
  191.8 2.2 constant_dynamic-update-slice_fusion.13
  195.1 2.2 constant_dynamic-update-slice_fusion.11
  197.2 2.1 constant_dynamic-update-slice_fusion.10
  199.4 2.1 constant_dynamic-update-slice_fusion.9
  201.5 5.0 collective-permute-done.6
  211.6 2.1 constant_dynamic-update-slice_fusion.3
  213.7 2.2 constant_dynamic-update-slice_fusion.2
  215.9 2.2 constant_dynamic-update-slice_fusion.1
  219.1 3.5 constant_dynamic-slice_fusion
  222.6 10.6 %fusion.68 = f32[4,12,128,1024]{3,2,1,0:T(8,128)} fusion(bf16[4,1024,12,64]{1,3,2,0:T(8,128)(2,1)S(1)} %bitcast.168, bf16[4,128,12,48]{1,3,2,0:T(8,128)(2,1)S(1)} %slice.110, bf16[4,128,12,16]{1,3,2,0:T(8,128)(2,1)S(1)} %copy-done.9), kind=kOutput, calls=%fused_computation.123 | convolution fusion | flops 806879232 | bytes 32243712 | tf_op jit(solution)/shard_map/sqhd,skhd->shqk/dot_general | solution.py:126
  233.2 12.8 %select_reduce_fusion.1 = (f32[4,12,128]{2,1,0:T(8,128)S(1)}, f32[4,12,128,1024]{3,2,1,0:T(8,128)}) fusion(pred[4,128,1024]{2,1,0:T(8,128)(4,1)S(1)} %fusion.26, bf16[4,1024,12,64]{1,3,2,0:T(8,128)(2,1)} %bitcast.166, bf16[4,128,12,48]{1,3,2,0:T(8,128)(2,1)S(1)} %slice.110, bf16[4,128,12,16]{1,3,2,0:T(8,128)(2,1)S(1)} %copy-done.9), kind=kOutput, calls=%fused_computation.7 | convolution fusion | flops 825747456 | bytes 32792576 | tf_op jit(solution)/shard_map/sqhd,skhd->shqk/dot_general | solution.py:126
  246.1 12.2 %select_reduce_fusion = f32[4,12,128]{2,1,0:T(8,128)S(1)} fusion(f32[4,12,128,1024]{3,2,1,0:T(8,128)} %get-tuple-element.76, f32[4,12,128]{2,1,0:T(8,128)S(1)} %broadcast_maximum_fusion, pred[4,128,1024]{2,1,0:T(8,128)(4,1)S(1)} %fusion.26), kind=kLoop, calls=%fused_computation.6 | loop fusion | flops 31451136 | bytes 25739264 | tf_op jit(solution)/shard_map/reduce_sum | solution.py:140
  258.4 14.1 %fusion.2 = f32[4,12,64,128]{3,2,1,0:T(8,128)} fusion(bf16[4,1024,12,64]{1,3,2,0:T(8,128)(2,1)} %bitcast.196, f32[4,12,128,1024]{3,2,1,0:T(8,128)} %fusion.68, f32[4,12,128]{2,1,0:T(8,128)S(1)} %log_add_fusion, pred[4,128,1024]{2,1,0:T(8,128)(4,1)S(1)} %fusion.26), kind=kOutput, calls=%fused_computation.10 | convolution fusion | flops 830472192 | bytes 33579008 | tf_op jit(solution)/shard_map/shqk,skhd->sqhd/dot_general | solution.py:152
  272.4 15.5 %fusion.29 = f32[4,128,12]{1,2,0:T(8,128)S(1)} fusion(f32[4,12,64,128]{3,2,1,0:T(8,128)} %fusion.2, bf16[4,1024,12,64]{1,3,2,0:T(8,128)(2,1)} %bitcast.197, f32[4,12,128,1024]{3,2,1,0:T(8,128)} %fusion.68, f32[4,12,128]{2,1,0:T(8,128)S(1)} %log_add_fusion, pred[4,128,1024]{2,1,0:T(8,128)(4,1)S(1)} %fusion.26, bf16[4,128,12,64]{1,0,3,2:T(4,128)(2,1)} %reshape.257), kind=kOutput, calls=%fused_computation.60 | convolution fusion | flops 850913280 | bytes 34390016 | tf_op jit(solution)/shard_map/shqk,skhd->sqhd/dot_general | solution.py:153
  287.9 20.4 %multiply_convert_fusion = bf16[4,12,128,1024]{3,2,1,0:T(8,128)(2,1)} fusion(f32[4,12,128,1024]{3,2,1,0:T(8,128)} %get-tuple-element.76, f32[4,12,128]{2,1,0:T(8,128)S(1)} %bitcast.200, f32[4,12,128]{2,1,0:T(8,128)S(1)} %log_add_fusion, pred[4,128,1024]{2,1,0:T(8,128)(4,1)S(1)} %fusion.26, bf16[4,1024,12,64]{1,3,2,0:T(8,128)(2,1)} %bitcast.198, ...), kind=kOutput, calls=%fused_computation.2 | convolution fusion | flops 843055104 | bytes 45400064 | tf_op jit(solution)/shard_map/sqhd,skhd->shqk/dot_general | solution.py:191
  308.3 10.9 %fusion.66 = f32[4,12,64,1024]{3,2,1,0:T(8,128)} fusion(bf16[4,12,128,1024]{3,2,1,0:T(8,128)(2,1)} %multiply_convert_fusion, bf16[4,128,12,48]{1,3,2,0:T(8,128)(2,1)S(1)} %slice.110, bf16[4,128,12,16]{1,3,2,0:T(8,128)(2,1)S(1)} %copy-done.9), kind=kOutput, calls=%fused_computation.121 | convolution fusion | flops 806879232 | bytes 25952256 | tf_op jit(solution)/shard_map/shqk,sqhd->skhd/dot_general | solution.py:198
  319.2 13.6 %fusion.4 = f32[4,12,64,1024]{3,2,1,0:T(8,128)} fusion(f32[4,12,128,1024]{3,2,1,0:T(8,128)} %get-tuple-element.76, f32[4,12,128]{2,1,0:T(8,128)S(1)} %log_add_fusion, pred[4,128,1024]{2,1,0:T(8,128)(4,1)S(1)} %fusion.26, bf16[4,128,12,64]{1,0,3,2:T(4,128)(2,1)S(1)} %copy-done.20), kind=kOutput, calls=%fused_computation.11 | convolution fusion | flops 830472192 | bytes 39084032 | tf_op jit(solution)/shard_map/shqk,sqhd->skhd/dot_general | solution.py:201
  332.9 18.7 %pad_maximum_fusion.1 = f32[4,1024,1536]{1,2,0:T(8,128)} fusion(f32[4,1024,768]{1,2,0:T(8,128)} %bitcast.165, f32[4,1024,768]{1,2,0:T(8,128)} %bitcast.164), kind=kLoop, calls=%fused_computation.1 | loop fusion | flops 6291456 | bytes 50331648 | tf_op jit(solution)/shard_map/concatenate | solution.py:204
  352.3 8.9 %all-gather = bf16[8,1,384]{2,1,0:T(2,128)(2,1)S(1)} all-gather(bf16[1,1,384]{2,1,0:T(2,128)(2,1)S(1)} %reshape.283), channel_id=1, replica_groups=mesh['rep'=4,'fsdp'=8] {'fsdp'}, dimensions={0}, use_global_device_ids=true | all-gather | bytes 6912 | tf_op jit(solution)/shard_map/all_gather | solution.py:83
  362.5 8.9 %fusion.93 = f32[512,3072]{1,0:T(8,128)} fusion(bf16[512,768]{1,0:T(8,128)(2,1)S(1)} %get-tuple-element.54, bf16[768,3072]{1,0:T(8,128)(2,1)} %all-gather.16.cloned.1.call-done), kind=kOutput, calls=%fused_computation.183 | convolution fusion | flops 2415919104 | bytes 11796480 | tf_op jit(solution)/shard_map/dot_general | solution.py:100
  371.4 19.3 %convert_reduce_fusion = (f32[3072]{0:T(1024)S(1)}, bf16[512,3072]{1,0:T(8,128)(2,1)S(1)}, f32[512,3072]{1,0:T(8,128)S(1)}) fusion(f32[512,3072]{1,0:T(8,128)} %fusion.93, f32[3072]{0:T(1024)S(1)} %bitcast.194, bf16[512,768]{1,0:T(8,128)(2,1)S(1)} %bitcast.177, bf16[768,3072]{1,0:T(8,128)(2,1)} %all-gather.18.cloned.1.call-done), kind=kOutput, calls=%fused_computation.24 | convolution fusion | flops 2533880832 | bytes 21258240 | tf_op jit(solution)/shard_map/dot_general | solution.py:174
  390.7 3.2 multiply_convert_fusion.1
  393.9 7.1 convolution_bitcast_fusion
  401.0 5.3 fusion.96
  406.3 11.6 %multiply_bitcast_fusion = f32[4,128,12,64]{1,3,2,0:T(8,128)S(1)} fusion(bf16[4,1024,12,64]{1,3,2,0:T(8,128)(2,1)} %bitcast.167, bf16[4,12,128,1024]{3,2,1,0:T(8,128)(2,1)} %multiply_convert_fusion), kind=kOutput, calls=%fused_computation.94 | convolution fusion | flops 805699584 | bytes 20447232 | tf_op jit(solution)/shard_map/shqk,skhd->sqhd/dot_general | solution.py:195
  417.9 2.1 convert_bitcast_fusion
  421.5 2.2 convolution_bitcast_fusion.1
  423.7 2.2 copy.57
  426.0 84.1 %reduce-scatter.3.cloned.1.call-done = f32[4,128,1536]{1,2,0:T(8,128)} async-done(((f32[4,1024,1536]{1,2,0:T(8,128)}), f32[4,128,1536]{1,2,0:T(8,128)}) %reduce-scatter.3.cloned.1.call-update) | async-done | bytes 3145744 | tf_op jit(solution)/shard_map/reduce_scatter | solution.py:211
  510.0 2.2 fusion.90
  514.2 2.2 copy.55
  517.9 4.9 fusion.22
  522.9 19.4 %pad_maximum_fusion = f32[768,9216]{1,0:T(8,128)} fusion(f32[768,3072]{1,0:T(8,128)} %convolution_bitcast_fusion, f32[768,3072]{1,0:T(8,128)} %fusion.96, f32[768,768]{1,0:T(8,128)S(1)} %copy.57, f32[768,2304]{1,0:T(8,128)} %fusion.22), kind=kLoop, calls=%fused_computation | loop fusion | flops 21233664 | bytes 56623104 | tf_op jit(solution)/shard_map/concatenate | solution.py:258
  543.1 172.6 %reduce-scatter.5.cloned.1.call-done = f32[96,9216]{1,0:T(8,128)} async-done(((f32[768,9216]{1,0:T(8,128)}), f32[96,9216]{1,0:T(8,128)}) %reduce-scatter.5.cloned.1.call-update) | async-done | bytes 3538960 | tf_op jit(solution)/shard_map/reduce_scatter | solution.py:257
  715.7 6.1 fusion.95
  721.8 5.8 fusion.94
  727.7 1.8 fusion.55
  729.6 5.3 fusion.86
  737.6 44.4 %all-reduce.18 = (f32[768]{0:T(1024)S(1)}, f32[768]{0:T(1024)S(1)}, f32[768]{0:T(1024)S(1)}, f32[768]{0:T(1024)S(1)}, f32[2304]{0:T(1024)S(1)}, /*index=5*/f32[768]{0:T(1024)S(1)}, f32[3072]{0:T(1024)S(1)}) all-reduce(f32[768]{0:T(1024)S(1)} %get-tuple-element.23, ...), channel_id=1, replica_groups=mesh['rep'=4,'fsdp'=8] {'rep','fsdp'}, use_global_device_ids=true, to_apply=%region_13.14 | all-reduce | flops 9216 | bytes 73728 | tf_op jit(solution)/shard_map/psum | solution.py:239
  785.7 3.0 add_convert_fusion.2
  788.7 64.2 %all-reduce.22.cloned.1.call-done = f32[96,9216]{1,0:T(8,128)} async-done(((f32[96,9216]{1,0:T(8,128)}), f32[96,9216]{1,0:T(8,128)}) %all-reduce.22.cloned.1.call-update) | async-done | bytes 3538960 | tf_op jit(solution)/shard_map/psum | solution.py:271
  852.9 3.3 fusion.89
  856.2 2.1 slice.88
  (192 shorter events, 49.1 us)
Async XLA Ops:
  7.2 42.0 %all-gather.8.cloned.1.call-start = ((), (), s32[]{:S(2)}) async-start(), calls=%async_computation.2 | async-start | bytes 3981312 | tf_op jit(solution)/shard_map/all_gather | solution.py:95
  7.9 164.0 %all-gather.14.cloned.1.call-start = ((), (), s32[]{:S(2)}) async-start(), calls=%async_computation.5 | async-start | bytes 1327104 | tf_op jit(solution)/shard_map/all_gather | solution.py:157
  8.7 224.6 %all-gather.12.cloned.1.call-start = ((), (), s32[]{:S(2)}) async-start(), calls=%async_computation.4 | async-start | bytes 7077888 | tf_op jit(solution)/shard_map/all_gather | solution.py:136
  10.0 45.3 %copy-start.31 = (f32[512]{0:T(512)}, f32[512]{0:T(512)S(1)}, u32[]{:S(2)}) copy-start(f32[512]{0:T(512)S(1)} %get-tuple-element.73) | copy-start | bytes 6148
  11.6 349.7 %copy-start.35 = (f32[4,128]{1,0:T(4,128)}, f32[4,128]{1,0:T(4,128)S(1)}, u32[]{:S(2)}) copy-start(f32[4,128]{1,0:T(4,128)S(1)} %fusion.41) | copy-start | bytes 6148
  12.5 58.2 %copy-start.23 = (f32[4,128,16]{1,2,0:T(8,128)}, f32[4,128,16]{1,2,0:T(8,128)S(1)}, u32[]{:S(2)}) copy-start(f32[4,128,16]{1,2,0:T(8,128)S(1)} %get-tuple-element.67) | copy-start | bytes 98308
  12.5 58.2 %copy-start.25 = (f32[4,128,16]{1,2,0:T(8,128)}, f32[4,128,16]{1,2,0:T(8,128)S(1)}, u32[]{:S(2)}) copy-start(f32[4,128,16]{1,2,0:T(8,128)S(1)} %get-tuple-element.68) | copy-start | bytes 98308
  47.5 313.7 %copy-start.27 = (f32[768]{0:T(1024)}, f32[768]{0:T(1024)S(1)}, u32[]{:S(2)}) copy-start(f32[768]{0:T(1024)S(1)} %convert_element_type.128) | copy-start | bytes 9220
  47.5 7.9 copy-start.29
  47.6 7.8 copy-start.33
  70.5 1.1 copy-start.8
  70.5 101.5 %copy-start.6 = (bf16[4,128,768]{2,1,0:T(8,128)(2,1)S(1)}, bf16[4,128,768]{2,1,0:T(8,128)(2,1)}, u32[]{:S(2)}) copy-start(bf16[4,128,768]{2,1,0:T(8,128)(2,1)} %param.17) | copy-start | bytes 2359300
  73.5 184.9 %all-gather.10.cloned.1.call-start = ((), (), s32[]{:S(2)}) async-start(), calls=%async_computation.3 | async-start | bytes 7077888 | tf_op jit(solution)/shard_map/all_gather | solution.py:144
  75.2 105.9 %copy-start.3 = (bf16[4,128,12,64]{1,3,2,0:T(8,128)(2,1)S(1)}, bf16[4,128,12,64]{1,3,2,0:T(8,128)(2,1)}, u32[]{:S(2)}) copy-start(bf16[4,128,12,64]{1,3,2,0:T(8,128)(2,1)} %pad_maximum_fusion.3) | copy-start | bytes 2359300
  76.3 286.2 %all-gather.16.cloned.1.call-start = ((), (), s32[]{:S(2)}) async-start(), calls=%async_computation.6 | async-start | bytes 5308416 | tf_op jit(solution)/shard_map/all_gather | solution.py:96
  76.9 294.5 %all-gather.18.cloned.1.call-start = ((), (), s32[]{:S(2)}) async-start(), calls=%async_computation.7 | async-start | bytes 5308416 | tf_op jit(solution)/shard_map/all_gather | solution.py:158
  77.0 16.4 %collective-permute-start = (bf16[4,128,768]{1,2,0:T(8,128)(2,1)}, bf16[4,128,768]{1,2,0:T(8,128)(2,1)S(1)}, u32[]{:S(2)}, u32[]{:S(2)}) collective-permute-start(bf16[4,128,768]{1,2,0:T(8,128)(2,1)} %bitcast.170), channel_id=1, source_target_pairs={{0,7},{1,0},{2,1},{3,2},{4,3},{5,4},{6,5},{7,6},{8,15},{9,8},{10,9... | collective-permute-start | bytes 2359304 | tf_op jit(solution)/shard_map/ppermute | solution.py:20
  93.3 78.2 %copy-start.10 = (bf16[4,128,768]{1,2,0:T(8,128)(2,1)}, bf16[4,128,768]{1,2,0:T(8,128)(2,1)S(1)}, u32[]{:S(2)}) copy-start(bf16[4,128,768]{1,2,0:T(8,128)(2,1)S(1)} %collective-permute-done) | copy-start | bytes 2359300
  93.3 12.3 %collective-permute-start.1 = (bf16[4,128,768]{1,2,0:T(8,128)(2,1)S(1)}, bf16[4,128,768]{1,2,0:T(8,128)(2,1)S(1)}, u32[]{:S(2)}, u32[]{:S(2)}) collective-permute-start(bf16[4,128,768]{1,2,0:T(8,128)(2,1)S(1)} %collective-permute-done), channel_id=1, source_target_pairs={{0,7},{1,0},{2,1},{3,2},{4,3},{5,4},{6,5},{7,6},{8,15},{9,8},{10,9... | collective-permute-start | bytes 2359304 | tf_op jit(solution)/shard_map/ppermute | solution.py:20
  105.6 0.9 copy-start.12
  106.5 28.9 %collective-permute-start.2 = (bf16[4,128,768]{1,2,0:T(8,128)(2,1)S(1)}, bf16[4,128,768]{1,2,0:T(8,128)(2,1)S(1)}, u32[]{:S(2)}, u32[]{:S(2)}) collective-permute-start(bf16[4,128,768]{1,2,0:T(8,128)(2,1)S(1)} %collective-permute-done.1), channel_id=1, source_target_pairs={{0,7},{1,0},{2,1},{3,2},{4,3},{5,4},{6,5},{7,6},{8,15},{9,8},{10,9... | collective-permute-start | bytes 2359304 | tf_op jit(solution)/shard_map/ppermute | solution.py:20
  135.4 0.9 copy-start.14
  136.3 12.3 %collective-permute-start.3 = (bf16[4,128,768]{1,2,0:T(8,128)(2,1)S(1)}, bf16[4,128,768]{1,2,0:T(8,128)(2,1)}, u32[]{:S(2)}, u32[]{:S(2)}) collective-permute-start(bf16[4,128,768]{1,2,0:T(8,128)(2,1)S(1)} %collective-permute-done.2), channel_id=1, source_target_pairs={{0,7},{1,0},{2,1},{3,2},{4,3},{5,4},{6,5},{7,6},{8,15},{9,8},{10,9... | collective-permute-start | bytes 2359304 | tf_op jit(solution)/shard_map/ppermute | solution.py:20
  148.6 19.9 %collective-permute-start.4 = (bf16[4,128,768]{1,2,0:T(8,128)(2,1)}, bf16[4,128,768]{1,2,0:T(8,128)(2,1)}, u32[]{:S(2)}, u32[]{:S(2)}) collective-permute-start(bf16[4,128,768]{1,2,0:T(8,128)(2,1)} %collective-permute-done.3), channel_id=1, source_target_pairs={{0,7},{1,0},{2,1},{3,2},{4,3},{5,4},{6,5},{7,6},{8,15},{9,8},{10,9... | collective-permute-start | bytes 2359304 | tf_op jit(solution)/shard_map/ppermute | solution.py:20
  151.6 358.5 %reduce-scatter.3.cloned.1.call-start = ((), (), s32[]{:S(2)}) async-start(), calls=%async_computation.8 | async-start | bytes 28311552 | tf_op jit(solution)/shard_map/reduce_scatter | solution.py:211
  168.5 18.4 %collective-permute-start.5 = (bf16[4,128,768]{1,2,0:T(8,128)(2,1)}, bf16[4,128,768]{1,2,0:T(8,128)(2,1)}, u32[]{:S(2)}, u32[]{:S(2)}) collective-permute-start(bf16[4,128,768]{1,2,0:T(8,128)(2,1)} %collective-permute-done.4), channel_id=1, source_target_pairs={{0,7},{1,0},{2,1},{3,2},{4,3},{5,4},{6,5},{7,6},{8,15},{9,8},{10,9... | collective-permute-start | bytes 2359304 | tf_op jit(solution)/shard_map/ppermute | solution.py:20
  179.6 14.4 %copy-start.15 = (bf16[4,128,768]{1,2,0:T(8,128)(2,1)S(1)}, bf16[4,128,768]{1,2,0:T(8,128)(2,1)}, u32[]{:S(2)}) copy-start(bf16[4,128,768]{1,2,0:T(8,128)(2,1)} %copy-done.14) | copy-start | bytes 2359300
  182.1 26.4 %copy-start.11 = (bf16[4,128,768]{1,2,0:T(8,128)(2,1)S(1)}, bf16[4,128,768]{1,2,0:T(8,128)(2,1)}, u32[]{:S(2)}) copy-start(bf16[4,128,768]{1,2,0:T(8,128)(2,1)} %copy-done.10) | copy-start | bytes 2359300
  186.8 19.6 %collective-permute-start.6 = (bf16[4,128,768]{1,2,0:T(8,128)(2,1)}, bf16[4,128,768]{1,2,0:T(8,128)(2,1)S(1)}, u32[]{:S(2)}, u32[]{:S(2)}) collective-permute-start(bf16[4,128,768]{1,2,0:T(8,128)(2,1)} %collective-permute-done.5), channel_id=1, source_target_pairs={{0,7},{1,0},{2,1},{3,2},{4,3},{5,4},{6,5},{7,6},{8,15},{9,8},{10,9... | collective-permute-start | bytes 2359304 | tf_op jit(solution)/shard_map/ppermute | solution.py:20
  191.8 17.7 %copy-start.13 = (bf16[4,128,768]{1,2,0:T(8,128)(2,1)S(1)}, bf16[4,128,768]{1,2,0:T(8,128)(2,1)}, u32[]{:S(2)}) copy-start(bf16[4,128,768]{1,2,0:T(8,128)(2,1)} %copy-done.12) | copy-start | bytes 2359300
  219.1 3.5 copy-start.9
  308.3 10.9 %copy-start.20 = (bf16[4,128,12,64]{1,0,3,2:T(4,128)(2,1)S(1)}, bf16[4,128,12,64]{1,0,3,2:T(4,128)(2,1)}, u32[]{:S(2)}) copy-start(bf16[4,128,12,64]{1,0,3,2:T(4,128)(2,1)} %reshape.257) | copy-start | bytes 2359300
  351.6 0.7 copy-start.39
  351.6 9.7 %copy-start = (bf16[4,128,768]{2,1,0:T(8,128)(2,1)S(1)}, bf16[4,128,768]{2,1,0:T(8,128)(2,1)}, u32[]{:S(2)}) copy-start(bf16[4,128,768]{2,1,0:T(8,128)(2,1)} %param.15) | copy-start | bytes 2359300
  351.6 364.1 %reduce-scatter.5.cloned.1.call-start = ((), (), s32[]{:S(2)}) async-start(), calls=%async_computation.9 | async-start | bytes 31850496 | tf_op jit(solution)/shard_map/reduce_scatter | solution.py:257
  371.4 19.3 %copy-start.2 = (f32[512,3072]{1,0:T(8,128)S(1)}, f32[512,3072]{1,0:T(8,128)}, u32[]{:S(2)}) copy-start(f32[512,3072]{1,0:T(8,128)} %fusion.93) | copy-start | bytes 18874372
  390.7 10.3 %copy-start.16 = (bf16[512,3072]{1,0:T(8,128)(2,1)}, bf16[512,3072]{1,0:T(8,128)(2,1)S(1)}, u32[]{:S(2)}) copy-start(bf16[512,3072]{1,0:T(8,128)(2,1)S(1)} %get-tuple-element.39) | copy-start | bytes 9437188
  417.9 2.8 copy-start.4
  420.6 0.9 copy-start.17
  423.7 88.5 %copy-start.26 = (f32[4,128,16]{1,2,0:T(8,128)S(1)}, f32[4,128,16]{1,2,0:T(8,128)}, u32[]{:S(2)}) copy-start(f32[4,128,16]{1,2,0:T(8,128)} %copy-done.25) | copy-start | bytes 98308
  426.0 86.7 %copy-start.24 = (f32[4,128,16]{1,2,0:T(8,128)S(1)}, f32[4,128,16]{1,2,0:T(8,128)}, u32[]{:S(2)}) copy-start(f32[4,128,16]{1,2,0:T(8,128)} %copy-done.23) | copy-start | bytes 98308
  510.0 2.4 copy-start.5
  512.3 1.3 slice-start
  513.7 4.2 copy-start.22
  516.5 1.4 copy-start.21
  542.2 0.7 copy-start.38
  542.2 0.7 copy-start.37
  542.3 310.6 %all-reduce.22.cloned.1.call-start = ((), (), s32[]{:S(2)}) async-start(), calls=%async_computation.10 | async-start | bytes 7077888 | tf_op jit(solution)/shard_map/psum | solution.py:271
  715.7 6.1 copy-start.19
  721.8 5.9 copy-start.1
  721.8 5.9 copy-start.18
  721.8 5.9 copy-start.40
  727.7 1.9 copy-start.28
  727.7 1.9 copy-start.30
  727.7 1.9 copy-start.32
  729.6 5.4 copy-start.36
  729.6 6.5 copy-start.34
  735.0 1.2 copy-start.7
  782.0 78.0 %copy-start.41 = (f32[96]{0:T(128)}, f32[96]{0:T(128)S(1)}, u32[]{:S(2)}) copy-start(f32[96]{0:T(128)S(1)} %dynamic_slice.31) | copy-start | bytes 1156
Sparse Core Ops, SparseCore 0:
  9.9 36.8 all-gather.7
  48.7 24.0 all-gather.13
  75.2 62.2 all-gather.11
  139.9 66.4 all-gather.9
  208.1 41.2 all-gather.15
  251.1 38.9 all-gather.17
  351.7 158.2 reduce-scatter.2
  542.4 173.2 reduce-scatter.4
  718.1 134.7 all-reduce.21
